TPU v7x, 32 devices: a whole 2x2x4 slice. The times are simulated.
32 devices in a mesh: tm: 4 (over x, core), slope: 8 (over z, y).
Axes of the slice: x: 2, y: 2, z: 4, core: 2. Of those that a mesh axis runs over, the one named last changes fastest.
Arguments:
- telemetry: bfloat16 [8, 128, 96, 4096], P('slope', None, None, 'tm'), may hold values from -24 to 24
- frame_ids: int32 [4096], P('tm'), may hold values from 0 to 1023, as said below
- valid: int32 [8, 48], replicated, may hold values 0 or 1
- noise: float32 [1024], replicated, may hold values from 0.1 to 1
- prior_next: float32 [8, 128, 96, 1024], P('slope', 'tm'), may hold values from -2 to 2
Outputs:
- panel: float32 [8, 128, 96, 1024], P('slope', 'tm')
- next_block: float32 [8, 128, 96, 1024], P('slope', 'tm')
Inputs may be any that keep to these rules, and one draw needn't show every extreme that they name: `frame_ids`: entry f names a frame of the block of 1024 buffer frames that starts at (f // 1024) * 1024; entries may repeat.
All inputs are finite; a program needn't handle non-finite values.
Results may differ from a plain program's by a relative error of at most 0.0003.
Values may be sent and summed in bfloat16 or wider, within the bound.
A program may use at most 256 MiB of HBM per device.

v0:
```python
import jax
import jax.numpy as jnp
from jax import lax
from jax.sharding import PartitionSpec as P


def shards(telemetry, frame_ids, valid, noise, prior_next):
    slope_count = lax.axis_size("slope")
    tm_count = lax.axis_size("tm")
    slope_index = lax.axis_index("slope")
    tm_index = lax.axis_index("tm")
    row_block = telemetry.shape[1]
    cycles = telemetry.shape[2]
    block_width = noise.shape[0]
    quarter = row_block // tm_count
    frames_total = frame_ids.shape[0] * tm_count
    rows_iota = lax.broadcasted_iota(jnp.int32, (row_block, cycles), 0)
    cycle_iota = lax.broadcasted_iota(jnp.int32, (row_block, cycles), 1)
    slope_ids = (cycle_iota * slope_count + slope_index) * row_block + rows_iota
    sensors, segments = valid.shape
    per_sensor = cycles * block_width // sensors
    seg_len = per_sensor // segments
    seg_codes = slope_ids // per_sensor * segments + slope_ids % per_sensor // seg_len
    labels = jnp.arange(sensors * segments, dtype=jnp.int32)
    keep_row = jnp.sum(jnp.where(seg_codes[:, :, None] == labels, valid.reshape(-1), 0), axis=2)
    selected = jnp.take(telemetry[0], frame_ids, axis=2) * keep_row[:, :, None].astype(jnp.bfloat16)
    first_cols = lax.all_gather(selected[:, 0, :], "slope", axis=0, tiled=True)
    gram_block = lax.psum_scatter(
        jnp.einsum("rcf,jf->rcj", selected, first_cols, preferred_element_type=jnp.float32),
        "tm",
        scatter_dimension=0,
        tiled=True,
    )
    diag_cols = lax.broadcasted_iota(jnp.int32, (quarter, block_width), 1)
    diag_ids = (
        slope_index * row_block
        + tm_index * quarter
        + lax.broadcasted_iota(jnp.int32, (quarter, block_width), 0)
    )
    first_block = gram_block / float(frames_total)
    first_block = first_block.at[:, 0, :].add(jnp.where(diag_cols == diag_ids, noise[None, :], 0.0))
    partial_gram = jnp.einsum(
        "rf,jf->rj", selected[:, 0, :], first_cols, preferred_element_type=jnp.float32
    )
    summed = lax.psum(partial_gram, "tm") / float(frames_total)
    full_cols = lax.broadcasted_iota(jnp.int32, (row_block, block_width), 1)
    own_ids = slope_index * row_block + lax.broadcasted_iota(jnp.int32, (row_block, block_width), 0)
    lead_rows = summed + jnp.where(full_cols == own_ids, noise[None, :], 0.0)
    diag_block = lax.all_gather(lead_rows, "slope", axis=0, tiled=True)
    factor = jnp.linalg.cholesky(diag_block)
    inverse = jax.scipy.linalg.solve_triangular(
        factor, jnp.eye(block_width, dtype=jnp.float32), lower=True
    )
    panel_rows = jnp.einsum("rcj,kj->rck", first_block, inverse, precision=lax.Precision.HIGHEST)
    second_part = lax.all_gather(panel_rows[:, 1, :], "tm", axis=0, tiled=True)
    second = lax.all_gather(second_part, "slope", axis=0, tiled=True)
    update = jnp.einsum("rci,ji->rcj", panel_rows, second, precision=lax.Precision.HIGHEST)
    next_block = prior_next[0] - update
    return (panel_rows[None], next_block[None])


def solution(mesh):
    return jax.shard_map(
        shards,
        mesh=mesh,
        in_specs=(P("slope", None, None, "tm"), P("tm"), P(), P(), P("slope", "tm", None, None)),
        out_specs=(P("slope", "tm", None, None), P("slope", "tm", None, None)),
        check_vma=False,
    )
```

profile of v0, /device:TPU:0, one launch (start us, length us, event | category | flops | bytes accessed | tf_op | source)
XLA Modules:
  0.0 851.8 jit_solution(15278420787638205463)
XLA Ops:
  9.5 4.9 select_reduce_fusion
  14.5 35.3 %copy.26 = bf16[1,128,96,1024]{1,2,3,0:T(8,128)(2,1)} copy(bf16[1,128,96,1024]{3,2,1,0:T(8,128)(2,1)} %param.7) | data formatting | bytes 50331648 | tf_op args[0]
  49.8 25.4 %gather_fusion = bf16[1024,128,96]{1,2,0:T(8,128)(2,1)} fusion(bf16[128,96,1024]{0,1,2:T(8,128)(2,1)} %bitcast.130, s32[1024]{0:T(1024)S(1)} %fusion.92), kind=kCustom, calls=%fused_computation | custom fusion | bytes 50335744 | tf_op jit(solution)/shard_map/jit(_take)/gather | solution.py:26
  75.2 32.4 %copy.27 = bf16[1024,128,96]{0,1,2:T(8,128)(2,1)} copy(bf16[1024,128,96]{1,2,0:T(8,128)(2,1)} %gather_fusion) | data formatting | bytes 50331648 | tf_op jit(solution)/shard_map/jit(_take)/gather | solution.py:26
  107.6 12.4 %multiply_bitcast_fusion = bf16[128,96,1024]{2,0,1:T(8,128)(2,1)S(1)} fusion(bf16[1024,128,96]{0,1,2:T(8,128)(2,1)} %copy.27, pred[1024]{0:T(1024)(128)(4,1)S(1)} %compare_and_fusion, bf16[128,96]{0,1:T(8,128)(2,1)S(1)} %convert_element_type.23), kind=kLoop, calls=%fused_computation.3 | loop fusion | flops 25165824 | bytes 50357248 | tf_op jit(solution)/shard_map/mul | solution.py:26
  120.1 8.3 copy-done
  129.1 52.1 %all-gather.9.cloned.1.call-done = bf16[1024,1,1024]{2,0,1:T(8,128)(2,1)} async-done(((bf16[128,1,1024]{2,0,1:T(8,128)(2,1)}), bf16[1024,1,1024]{2,0,1:T(8,128)(2,1)}) %all-gather.9.cloned.1.call-update) | async-done | bytes 2097168 | tf_op jit(solution)/shard_map/all_gather | solution.py:27
  181.2 3.3 fusion.20
  184.7 31.8 %all-reduce.3.cloned.1.call-done = f32[128,1024]{0,1:T(8,128)} async-done(((f32[128,1024]{0,1:T(8,128)}), f32[128,1024]{0,1:T(8,128)}) %all-reduce.3.cloned.1.call-update) | async-done | bytes 524304 | tf_op jit(solution)/shard_map/psum | solution.py:45
  219.0 36.4 %fusion.18 = f32[128,96,1024]{2,0,1:T(8,128)} fusion(bf16[128,96,1024]{2,0,1:T(8,128)(2,1)} %copy-done, bf16[1024,1,1024]{2,0,1:T(8,128)(2,1)S(1)} %copy-done.3), kind=kOutput, calls=%fused_computation.28 | convolution fusion | flops 25769803776 | bytes 77594624 | tf_op jit(solution)/shard_map/rcf,jf->rcj/dot_general | solution.py:29
  255.9 2.4 fusion.34
  258.3 35.8 %all-gather.7.cloned.1.call-done = f32[1024,1024]{0,1:T(8,128)} async-done(((f32[128,1024]{0,1:T(8,128)}), f32[1024,1024]{0,1:T(8,128)}) %all-gather.7.cloned.1.call-update) | async-done | bytes 4194320 | tf_op jit(solution)/shard_map/all_gather | solution.py:49
  294.1 5.5 copy.30
  299.6 5.7 fusion.7
  305.3 2.5 copy-done.2
  307.8 11.7 %cholesky.223 = f32[128,128]{1,0:T(8,128)S(1)} custom-call(f32[128,128]{1,0:T(8,128)S(1)} %cholesky.580), custom_call_target="Cholesky" | custom-call | tf_op jit(solution)/shard_map/jit(cholesky)/cholesky | solution.py:50
  319.5 9.8 %custom-call.63 = f32[1,128,128]{1,2,0:T(8,128)S(1)} custom-call(f32[1,128,128]{2,1,0:T(8,128)S(1)} %get-tuple-element.78), custom_call_target="InvertDiagBlocksLowerTriangular" | custom-call | tf_op jit(solution)/shard_map/jit(cholesky)/cholesky | solution.py:50
  329.4 3.1 cholesky.255
  332.5 2.4 constant_dynamic-update-slice_fusion.32
  336.5 11.9 %cholesky.244 = f32[128,128]{1,0:T(8,128)S(1)} custom-call(f32[128,128]{1,0:T(8,128)S(1)} %cholesky.584), custom_call_target="Cholesky" | custom-call | tf_op jit(solution)/shard_map/jit(cholesky)/cholesky | solution.py:50
  349.0 9.8 %custom-call.64 = f32[1,128,128]{1,2,0:T(8,128)S(1)} custom-call(f32[1,128,128]{2,1,0:T(8,128)S(1)} %get-tuple-element.75), custom_call_target="InvertDiagBlocksLowerTriangular" | custom-call | tf_op jit(solution)/shard_map/jit(cholesky)/cholesky | solution.py:50
  362.2 11.7 %cholesky.468 = f32[128,128]{1,0:T(8,128)S(1)} custom-call(f32[128,128]{1,0:T(8,128)S(1)} %cholesky.589), custom_call_target="Cholesky" | custom-call | tf_op jit(solution)/shard_map/jit(cholesky)/cholesky | solution.py:50
  374.5 9.8 %custom-call.65 = f32[1,128,128]{1,2,0:T(8,128)S(1)} custom-call(f32[1,128,128]{2,1,0:T(8,128)S(1)} %get-tuple-element.72), custom_call_target="InvertDiagBlocksLowerTriangular" | custom-call | tf_op jit(solution)/shard_map/jit(cholesky)/cholesky | solution.py:50
  385.5 2.4 convolution_subtract_fusion.7
  387.9 12.1 %cholesky.487 = f32[128,128]{1,0:T(8,128)S(1)} custom-call(f32[128,128]{1,0:T(8,128)S(1)} %cholesky.594), custom_call_target="Cholesky" | custom-call | tf_op jit(solution)/shard_map/jit(cholesky)/cholesky | solution.py:50
  400.6 9.8 %custom-call.66 = f32[1,128,128]{1,2,0:T(8,128)S(1)} custom-call(f32[1,128,128]{2,1,0:T(8,128)S(1)} %get-tuple-element.69), custom_call_target="InvertDiagBlocksLowerTriangular" | custom-call | tf_op jit(solution)/shard_map/jit(cholesky)/cholesky | solution.py:50
  411.5 2.4 convolution_subtract_fusion.8
  413.9 11.7 %cholesky.506 = f32[128,128]{1,0:T(8,128)S(1)} custom-call(f32[128,128]{1,0:T(8,128)S(1)} %cholesky.599), custom_call_target="Cholesky" | custom-call | tf_op jit(solution)/shard_map/jit(cholesky)/cholesky | solution.py:50
  426.2 9.9 %custom-call.67 = f32[1,128,128]{1,2,0:T(8,128)S(1)} custom-call(f32[1,128,128]{2,1,0:T(8,128)S(1)} %get-tuple-element.66), custom_call_target="InvertDiagBlocksLowerTriangular" | custom-call | tf_op jit(solution)/shard_map/jit(cholesky)/cholesky | solution.py:50
  439.5 11.7 %cholesky.526 = f32[128,128]{1,0:T(8,128)S(1)} custom-call(f32[128,128]{1,0:T(8,128)S(1)} %cholesky.604), custom_call_target="Cholesky" | custom-call | tf_op jit(solution)/shard_map/jit(cholesky)/cholesky | solution.py:50
  451.8 9.8 %custom-call.68 = f32[1,128,128]{1,2,0:T(8,128)S(1)} custom-call(f32[1,128,128]{2,1,0:T(8,128)S(1)} %get-tuple-element.63), custom_call_target="InvertDiagBlocksLowerTriangular" | custom-call | tf_op jit(solution)/shard_map/jit(cholesky)/cholesky | solution.py:50
  464.6 11.7 %cholesky.546 = f32[128,128]{1,0:T(8,128)S(1)} custom-call(f32[128,128]{1,0:T(8,128)S(1)} %cholesky.609), custom_call_target="Cholesky" | custom-call | tf_op jit(solution)/shard_map/jit(cholesky)/cholesky | solution.py:50
  477.0 9.8 %custom-call.69 = f32[1,128,128]{1,2,0:T(8,128)S(1)} custom-call(f32[1,128,128]{2,1,0:T(8,128)S(1)} %get-tuple-element.60), custom_call_target="InvertDiagBlocksLowerTriangular" | custom-call | tf_op jit(solution)/shard_map/jit(cholesky)/cholesky | solution.py:50
  489.5 11.7 %cholesky.564 = f32[128,128]{1,0:T(8,128)S(1)} custom-call(f32[128,128]{1,0:T(8,128)S(1)} %convolution_subtract_fusion.11), custom_call_target="Cholesky" | custom-call | tf_op jit(solution)/shard_map/jit(cholesky)/cholesky | solution.py:50
  511.7 5.0 select_select_fusion
  516.6 24.2 %while.2 = (s32[]{:T(128)}, f32[1024,1024]{1,0:T(8,128)}, s32[8,2]{0,1:T(2,128)S(1)}, f32[8,128,128]{2,1,0:T(8,128)S(1)}, s32[]{:T(128)}) while((s32[]{:T(128)}, f32[1024,1024]{1,0:T(8,128)}, s32[8,2]{0,1:T(2,128)S(1)}, f32[8,128,128]{2,1,0:T(8,128)S(1)}, s32[]{:T(128)}) %tuple.65), condition=%wide.while_cond.1, body=%wide.while_body.1.sunk | while | flops 2 | bytes 131189 | solution.py:51
  526.4 2.4 bitcast_dynamic-update-slice_fusion.2
  535.5 2.4 bitcast_dynamic-update-slice_fusion.2
  540.8 78.8 %custom-call.70 = f32[8,128,128]{1,2,0:T(8,128)S(1)} custom-call(f32[8,128,128]{2,1,0:T(8,128)S(1)} %get-tuple-element.21), custom_call_target="InvertDiagBlocksLowerTriangular" | custom-call | tf_op jit(solution)/shard_map/jit(_solve_triangular)/triangular_solve | solution.py:51
  634.9 2.6 convolution_subtract_fusion.2
  639.0 2.8 convolution_subtract_fusion.1
  643.3 3.3 convolution_subtract_fusion.3
  648.0 12.4 %broadcast_multiply_fusion = f32[32,96,1024]{2,0,1:T(8,128)} fusion(f32[32,96,1024]{2,0,1:T(8,128)} %reduce-scatter.2.cloned.1.call-done), kind=kLoop, calls=%fused_computation.10 | loop fusion | flops 3145728 | bytes 25165824 | tf_op jit(solution)/shard_map/div | solution.py:40
  662.0 52.3 %fusion.1 = f32[32,96,1024]{2,1,0:T(8,128)S(1)} fusion(f32[32,96,1024]{2,0,1:T(8,128)} %fusion.65, f32[1024,1024]{1,0:T(8,128)} %convolution_dynamic-update-slice_fusion), kind=kOutput, calls=%fused_computation.8 | convolution fusion | flops 38654705664 | bytes 29360128 | tf_op jit(solution)/shard_map/rcj,kj->rck/dot_general | solution.py:54
  714.2 4.8 copy-done.5
  719.1 7.8 all-gather.1
  727.0 71.3 %all-gather.11.cloned.1.call-done = f32[1024,1,1024]{2,1,0:T(1,128)} async-done(((f32[128,1,1024]{2,1,0:T(1,128)}), f32[1024,1,1024]{2,1,0:T(1,128)}) %all-gather.11.cloned.1.call-update) | async-done | bytes 4194320 | tf_op jit(solution)/shard_map/all_gather | solution.py:56
  798.4 46.7 %fusion = f32[1,32,96,1024]{3,2,1,0:T(8,128)} fusion(f32[1,32,96,1024]{3,2,1,0:T(8,128)} %param.11, f32[32,96,1024]{2,1,0:T(8,128)} %copy-done.5, f32[1024,1,1024]{2,1,0:T(1,128)} %all-gather.11.cloned.1.call-done), kind=kOutput, calls=%fused_computation.7 | convolution fusion | flops 38657851392 | bytes 41943040 | tf_op jit(solution)/shard_map/rci,ji->rcj/dot_general | solution.py:57
  (104 shorter events, 72.0 us)
Async XLA Ops:
  7.2 174.1 %all-gather.9.cloned.1.call-start = ((), (), s32[]{:S(2)}) async-start(), calls=%async_computation.4 | async-start | bytes 2359296 | tf_op jit(solution)/shard_map/all_gather | solution.py:27
  120.0 8.3 copy-start
  128.3 88.1 %copy-start.4 = (f32[1024]{0:T(1024)S(1)}, f32[1024]{0:T(1024)}, u32[]{:S(2)}) copy-start(f32[1024]{0:T(1024)} %param.10) | copy-start | bytes 12292
  129.1 87.3 %all-reduce.3.cloned.1.call-start = ((), (), s32[]{:S(2)}) async-start(), calls=%async_computation.2 | async-start | bytes 1048576 | tf_op jit(solution)/shard_map/psum | solution.py:45
  181.2 37.8 %copy-start.3 = (bf16[1024,1,1024]{2,0,1:T(8,128)(2,1)S(1)}, bf16[1024,1,1024]{2,0,1:T(8,128)(2,1)}, u32[]{:S(2)}) copy-start(bf16[1024,1,1024]{2,0,1:T(8,128)(2,1)} %all-gather.9.cloned.1.call-done) | copy-start | bytes 6291460
  184.6 109.5 %all-gather.7.cloned.1.call-start = ((), (), s32[]{:S(2)}) async-start(), calls=%async_computation.3 | async-start | bytes 4718592 | tf_op jit(solution)/shard_map/all_gather | solution.py:49
  218.5 429.5 %reduce-scatter.2.cloned.1.call-start = ((), (), s32[]{:S(2)}) async-start(), calls=%async_computation.1 | async-start | bytes 62914560 | tf_op jit(solution)/shard_map/reduce_scatter | solution.py:28
  255.5 542.9 %all-gather.11.cloned.1.call-start = ((), (), s32[]{:S(2)}) async-start(), calls=%async_computation.5 | async-start | bytes 4718592 | tf_op jit(solution)/shard_map/all_gather | solution.py:56
  305.3 2.5 copy-start.2
  619.6 4.8 copy-start.1
  714.2 4.8 copy-start.5
Sparse Core Ops, SparseCore 0:
  129.2 51.9 all-gather.8
  184.7 31.6 all-reduce.2
  219.1 75.0 all-gather.6
  296.6 341.3 reduce-scatter.1
  727.1 71.1 all-gather.10
where the time goes:
time: 858 us; the launch traced here: 852 us
  other arithmetic  299 us (35%)
  waiting for transfers between devices  191 us (22%)
  matrix products  190 us (22%)
  local copies, waits for them, and re-layouts  143 us (17%)
  between operations  19.6 us (2%)
    another operation x30, other arithmetic, shards(): factor = jnp.linalg.cholesky(diag_block)  172 us
    another operation x3, other arithmetic, shards(): jax.scipy.linalg.solve_triangular(factor, jnp.eye(block_width, dtype=jnp....  83.8 us
    all_gather x1, waiting for transfers between devices, shards(): second = lax.all_gather(second_part, 'slope', axis=0, tiled=True)  71.3 us
    gather x2, local copies, waits for them, and re-layouts, shards(): jnp.take(telemetry[0], frame_ids, axis=2)  57.8 us
    dot_general x1, matrix products, shards(): jnp.einsum('rcj,kj->rck', first_block, inverse, precision=lax.Precision.H...  52.3 us
    all_gather x1, waiting for transfers between devices, shards(): first_cols = lax.all_gather(selected[:, 0, :], 'slope', axis=0, tiled=True)  52.1 us
    unnamed x13, local copies, waits for them, and re-layouts  50.9 us
    dot_general x1, matrix products, shards(): jnp.einsum('rci,ji->rcj', panel_rows, second, precision=lax.Precision.HIG...  46.7 us
  transfers between devices with their start and end apart: 5, of which 4 were waited for; matrix products, arithmetic and copies ran while one was open for 45% of the time, Pallas kernels for 0%

commit v1 on v0

v1 whole, which is shorter than its diff:
```python
import jax
import jax.numpy as jnp
from jax import lax
from jax.sharding import PartitionSpec as P


def dot_hi(a, b, dims):
    return lax.dot_general(
        a, b, (dims, ((), ())), precision=lax.Precision.HIGHEST, preferred_element_type=jnp.float32
    )


def block_inverse(diag_block, size):
    width = diag_block.shape[0]
    steps = width // size
    eye = jnp.eye(size, dtype=jnp.float32)
    trail = diag_block
    inv_rows = []
    low_cols = []
    for step in range(steps):
        pivot = trail[:size, :size]
        low = lax.linalg.cholesky(pivot, symmetrize_input=False)
        low_inv = lax.linalg.triangular_solve(low, eye, left_side=True, lower=True)
        base = step * size
        if step == 0:
            inv_row = low_inv
        else:
            left = jnp.concatenate(
                [c[base - (k + 1) * size : base - (k + 1) * size + size] for k, c in enumerate(low_cols)], axis=1
            )
            stacked = jnp.concatenate(inv_rows, axis=0)[:, :base]
            part = dot_hi(left, stacked, ((1,), (0,)))
            inv_row = jnp.concatenate([-dot_hi(low_inv, part, ((1,), (0,))), low_inv], axis=1)
        inv_rows.append(jnp.pad(inv_row, ((0, 0), (0, width - base - size))))
        if step + 1 < steps:
            col = dot_hi(trail[size:, :size], low_inv, ((1,), (1,)))
            low_cols.append(col)
            trail = trail[size:, size:] - dot_hi(col, col, ((1,), (1,)))
    return jnp.concatenate(inv_rows, axis=0)


def shards(telemetry, frame_ids, valid, noise, prior_next):
    slope_count = lax.axis_size("slope")
    tm_count = lax.axis_size("tm")
    slope_index = lax.axis_index("slope")
    tm_index = lax.axis_index("tm")
    row_block = telemetry.shape[1]
    cycles = telemetry.shape[2]
    frames_dev = telemetry.shape[3]
    block_width = noise.shape[0]
    quarter = row_block // tm_count
    frames_total = frame_ids.shape[0] * tm_count
    rows_iota = lax.broadcasted_iota(jnp.int32, (row_block, cycles), 0)
    cycle_iota = lax.broadcasted_iota(jnp.int32, (row_block, cycles), 1)
    slope_ids = (cycle_iota * slope_count + slope_index) * row_block + rows_iota
    sensors, segments = valid.shape
    per_sensor = cycles * block_width // sensors
    seg_len = per_sensor // segments
    seg_codes = slope_ids // per_sensor * segments + slope_ids % per_sensor // seg_len
    labels = jnp.arange(sensors * segments, dtype=jnp.int32)
    keep_row = jnp.sum(jnp.where(seg_codes[:, :, None] == labels, valid.reshape(-1), 0), axis=2).astype(jnp.float32)

    lead = telemetry[0, :, 0, :] * keep_row[:, 0:1].astype(jnp.bfloat16)
    first_raw = lax.all_gather(lead, "slope", axis=0, tiled=True)
    slots = lax.broadcasted_iota(jnp.int32, (frame_ids.shape[0], frames_dev), 1)
    counts = jnp.sum((frame_ids[:, None] == slots).astype(jnp.float32), axis=0)
    weighted = first_raw.astype(jnp.float32) * (counts / float(frames_total))[None, :]
    coarse = lax.reduce_precision(weighted, exponent_bits=8, mantissa_bits=7)
    high = coarse.astype(jnp.bfloat16)
    low = (weighted - coarse).astype(jnp.bfloat16)
    own = lax.dynamic_slice_in_dim(first_raw, slope_index * row_block, row_block, axis=0)

    def gram(rows, dims):
        return lax.dot_general(rows, high, (dims, ((), ())), preferred_element_type=jnp.float32) + lax.dot_general(
            rows, low, (dims, ((), ())), preferred_element_type=jnp.float32
        )

    full_cols = lax.broadcasted_iota(jnp.int32, (row_block, block_width), 1)
    own_ids = slope_index * row_block + lax.broadcasted_iota(jnp.int32, (row_block, block_width), 0)
    summed = lax.psum(gram(own, ((1,), (1,))), "tm")
    lead_rows = summed + jnp.where(full_cols == own_ids, noise[None, :], 0.0)
    diag_block = lax.all_gather(lead_rows, "slope", axis=0, tiled=True)

    partial = gram(telemetry[0], ((2,), (1,))) * keep_row[:, :, None]
    gram_block = lax.psum_scatter(partial, "tm", scatter_dimension=0, tiled=True)

    inverse = block_inverse(diag_block, 128)

    diag_cols = lax.broadcasted_iota(jnp.int32, (quarter, block_width), 1)
    diag_ids = (
        slope_index * row_block
        + tm_index * quarter
        + lax.broadcasted_iota(jnp.int32, (quarter, block_width), 0)
    )
    first_block = gram_block.at[:, 0, :].add(jnp.where(diag_cols == diag_ids, noise[None, :], 0.0))
    next_rows = dot_hi(first_block[:, 1, :], inverse, ((1,), (1,)))
    second = lax.all_gather(next_rows, ("slope", "tm"), axis=0, tiled=True)
    panel_rows = lax.dot_general(
        first_block, inverse, (((2,), (1,)), ((), ())),
        precision=lax.Precision.HIGHEST, preferred_element_type=jnp.float32,
    )
    update = lax.dot_general(
        panel_rows, second, (((2,), (1,)), ((), ())),
        precision=lax.Precision.HIGH, preferred_element_type=jnp.float32,
    )
    return (panel_rows[None], (prior_next[0] - update)[None])


def solution(mesh):
    return jax.shard_map(
        shards,
        mesh=mesh,
        in_specs=(P("slope", None, None, "tm"), P("tm"), P(), P(), P("slope", "tm", None, None)),
        out_specs=(P("slope", "tm", None, None), P("slope", "tm", None, None)),
        check_vma=False,
    )
```

time: 858 us -> 736 us (0.86)
  other arithmetic: 299 us -> 202 us
  local copies, waits for them, and re-layouts: 143 us -> 84.5 us
  matrix products: 190 us -> 234 us
    reduce_scatter x1, waiting for transfers between devices: 0.01 us -> 108 us  [shards(): lax.psum_scatter(partial, 'tm', scatter_dimension=0, tiled=True)]
    dot_general x4 -> x35, matrix products: 139 us -> 232 us  [the longest x2 55.8 us: gram(): lax.dot_general(rows, high, (dims, ((), ())), preferred_element_type=jnp....]
    all_gather x2, waiting for transfers between devices: 123 us -> 50.9 us  [the longest x1 50.9 us: shards(): first_raw = lax.all_gather(lead, 'slope', axis=0, tiled=True)]
    another operation x33 -> x40, other arithmetic: 256 us -> 184 us  [the longest x24 99.9 us: block_inverse(): low = lax.linalg.cholesky(pivot, symmetrize_input=False)]
    gather x2 -> x0, local copies, waits for them, and re-layouts: 57.8 us -> none  [shards(): jnp.take(telemetry[0], frame_ids, axis=2)]
    another operation x29 -> x8, matrix products: 51.5 us -> 2.14 us  [block_inverse(): low_inv = lax.linalg.triangular_solve(low, eye, left_side=True, lower=True)]
    mul x0 -> x1, local copies, waits for them, and re-layouts: none -> 49.2 us  [shards(): partial = gram(telemetry[0], ((2,), (1,))) * keep_row[:, :, None]]
    all_gather x1, waiting for transfers between devices: 35.8 us -> 0.02 us  [shards(): diag_block = lax.all_gather(lead_rows, 'slope', axis=0, tiled=True)]
  transfers between devices with their start and end apart: 5 -> 5, of which waited for: 4 -> 3; matrix products, arithmetic and copies ran while one was open for 45% -> 63% of each run, Pallas kernels for 0% -> 0%
where the time goes in v1:
time: 736 us; the launch traced here: 727 us
  matrix products  234 us (32%)
  other arithmetic  202 us (27%)
  waiting for transfers between devices  190 us (26%)
  local copies, waits for them, and re-layouts  84.5 us (11%)
  between operations  15 us (2%)
    reduce_scatter x1, waiting for transfers between devices, shards(): lax.psum_scatter(partial, 'tm', scatter_dimension=0, tiled=True)  108 us
    another operation x24, other arithmetic, block_inverse(): low = lax.linalg.cholesky(pivot, symmetrize_input=False)  99.9 us
    another operation x16, other arithmetic, block_inverse(): low_inv = lax.linalg.triangular_solve(low, eye, left_side=True, lower=True)  84.3 us
    dot_general x2, matrix products, gram(): lax.dot_general(rows, high, (dims, ((), ())), preferred_element_type=jnp....  55.8 us
    dot_general x2, matrix products, gram(): lax.dot_general(rows, low, (dims, ((), ())), preferred_element_type=jnp.f...  53.3 us
    dot_general x1, matrix products, shards(): lax.dot_general(first_block, inverse, (((2,), (1,)), ((), ())), precision...  52.5 us
    all_gather x1, waiting for transfers between devices, shards(): first_raw = lax.all_gather(lead, 'slope', axis=0, tiled=True)  50.9 us
    mul x1, local copies, waits for them, and re-layouts, shards(): partial = gram(telemetry[0], ((2,), (1,))) * keep_row[:, :, None]  49.2 us
  transfers between devices with their start and end apart: 5, of which 3 were waited for; matrix products, arithmetic and copies ran while one was open for 63% of the time, Pallas kernels for 0%

profile of v1, /device:TPU:0, one launch (start us, length us, event | category | flops | bytes accessed | tf_op | source)
XLA Modules:
  0.0 726.6 jit_solution(14233730240348588279)
XLA Ops:
  7.2 2.0 slice.199
  10.1 4.9 select_reduce_fusion
  16.0 1.2 convert_reduce_fusion
  17.2 50.9 %all-gather.4.cloned.1.call-done = bf16[1024,1024]{1,0:T(8,128)(2,1)} async-done(((bf16[128,1024]{1,0:T(8,128)(2,1)}), bf16[1024,1024]{1,0:T(8,128)(2,1)}) %all-gather.4.cloned.1.call-update) | async-done | bytes 2097168 | tf_op jit(solution)/shard_map/all_gather | solution.py:64
  68.1 2.7 fusion.27
  70.9 1.6 fusion.30
  72.7 31.7 %all-reduce.9.cloned.1.call-done = f32[128,1024]{1,0:T(8,128)} async-done(((f32[128,1024]{1,0:T(8,128)}), f32[128,1024]{1,0:T(8,128)}) %all-reduce.9.cloned.1.call-update) | async-done | bytes 524304 | tf_op jit(solution)/shard_map/psum | solution.py:80
  104.4 2.0 select_add_fusion
  106.4 50.6 %fusion = f32[1024,128,96]{1,0,2:T(8,128)} fusion(bf16[128,96,1024]{2,1,0:T(8,128)(2,1)} %bitcast.117, bf16[1024,1024]{1,0:T(8,128)(2,1)S(1)} %copy-done.20, f32[1024]{0:T(1024)S(1)} %broadcast_multiply_fusion), kind=kOutput, calls=%fused_computation.1 | convolution fusion | flops 25775046656 | bytes 77598720 | tf_op jit(solution)/shard_map/dot_general | solution.py:74
  157.0 54.1 %multiply_bitcast_fusion = f32[128,96,1024]{0,2,1:T(8,128)} fusion(f32[1024,128,96]{1,0,2:T(8,128)} %fusion, f32[128,96]{0,1:T(8,128)S(1)} %copy.64, bf16[128,96,1024]{2,1,0:T(8,128)(2,1)} %bitcast.118, bf16[1024,1024]{1,0:T(8,128)(2,1)S(1)} %copy-done.20, f32[1024]{0:T(1024)S(1)} %broadcast_multiply_fusion), kind=kOutput, calls=%fused_computation | convolution fusion | flops 25799163904 | bytes 127979520 | tf_op jit(solution)/shard_map/dot_general | solution.py:74
  211.2 49.2 %copy.65 = f32[128,96,1024]{2,1,0:T(8,128)} copy(f32[128,96,1024]{0,2,1:T(8,128)} %multiply_bitcast_fusion) | data formatting | bytes 100663296 | tf_op jit(solution)/shard_map/mul | solution.py:84
  261.7 11.7 %custom-call.20 = f32[128,128]{1,0:T(8,128)S(1)} custom-call(f32[128,128]{1,0:T(8,128)S(1)} %slice.259), custom_call_target="Cholesky" | custom-call | tf_op jit(solution)/shard_map/cholesky/custom-call.1 | solution.py:22
  274.8 9.8 %custom-call.21 = f32[1,128,128]{1,2,0:T(8,128)S(1)} custom-call(f32[1,128,128]{2,1,0:T(8,128)S(1)} %fusion.96), custom_call_target="InvertDiagBlocksLowerTriangular" | custom-call | tf_op jit(solution)/shard_map/triangular_solve/custom-call.0 | solution.py:23
  284.9 1.7 fusion.35
  286.7 5.6 slice_subtract_fusion
  292.3 11.9 %custom-call.22 = f32[128,128]{1,0:T(8,128)S(1)} custom-call(f32[128,128]{1,0:T(8,128)S(1)} %slice.262), custom_call_target="Cholesky" | custom-call | tf_op jit(solution)/shard_map/cholesky/custom-call.1 | solution.py:22
  305.5 9.8 %custom-call.23 = f32[1,128,128]{1,2,0:T(8,128)S(1)} custom-call(f32[1,128,128]{2,1,0:T(8,128)S(1)} %fusion.97), custom_call_target="InvertDiagBlocksLowerTriangular" | custom-call | tf_op jit(solution)/shard_map/triangular_solve/custom-call.0 | solution.py:23
  316.9 2.1 slice_subtract_fusion.1
  319.0 1.4 copy-done
  320.4 11.7 %custom-call.24 = f32[128,128]{1,0:T(8,128)S(1)} custom-call(f32[128,128]{1,0:T(8,128)S(1)} %slice.266), custom_call_target="Cholesky" | custom-call | tf_op jit(solution)/shard_map/cholesky/custom-call.1 | solution.py:22
  333.4 10.0 %custom-call.25 = f32[1,128,128]{1,2,0:T(8,128)S(1)} custom-call(f32[1,128,128]{2,1,0:T(8,128)S(1)} %fusion.98), custom_call_target="InvertDiagBlocksLowerTriangular" | custom-call | tf_op jit(solution)/shard_map/triangular_solve/custom-call.0 | solution.py:23
  344.4 1.5 fusion.41
  345.9 2.9 slice_subtract_fusion.2
  348.8 11.7 %custom-call.26 = f32[128,128]{1,0:T(8,128)S(1)} custom-call(f32[128,128]{1,0:T(8,128)S(1)} %slice.271), custom_call_target="Cholesky" | custom-call | tf_op jit(solution)/shard_map/cholesky/custom-call.1 | solution.py:22
  361.9 9.8 %custom-call.27 = f32[1,128,128]{1,2,0:T(8,128)S(1)} custom-call(f32[1,128,128]{2,1,0:T(8,128)S(1)} %fusion.99), custom_call_target="InvertDiagBlocksLowerTriangular" | custom-call | tf_op jit(solution)/shard_map/triangular_solve/custom-call.0 | solution.py:23
  373.1 1.1 convolution_subtract_fusion
  375.2 12.1 %custom-call.28 = f32[128,128]{1,0:T(8,128)S(1)} custom-call(f32[128,128]{1,0:T(8,128)S(1)} %slice.277), custom_call_target="Cholesky" | custom-call | tf_op jit(solution)/shard_map/cholesky/custom-call.1 | solution.py:22
  388.6 9.8 %custom-call.29 = f32[1,128,128]{1,2,0:T(8,128)S(1)} custom-call(f32[1,128,128]{2,1,0:T(8,128)S(1)} %fusion.100), custom_call_target="InvertDiagBlocksLowerTriangular" | custom-call | tf_op jit(solution)/shard_map/triangular_solve/custom-call.0 | solution.py:23
  399.5 1.3 fusion.80
  400.8 1.8 convolution_subtract_fusion.1
  402.6 11.7 %custom-call.30 = f32[128,128]{1,0:T(8,128)S(1)} custom-call(f32[128,128]{1,0:T(8,128)S(1)} %slice.284), custom_call_target="Cholesky" | custom-call | tf_op jit(solution)/shard_map/cholesky/custom-call.1 | solution.py:22
  415.7 9.8 %custom-call.31 = f32[1,128,128]{1,2,0:T(8,128)S(1)} custom-call(f32[1,128,128]{2,1,0:T(8,128)S(1)} %fusion.101), custom_call_target="InvertDiagBlocksLowerTriangular" | custom-call | tf_op jit(solution)/shard_map/triangular_solve/custom-call.0 | solution.py:23
  427.2 11.9 %custom-call.32 = f32[128,128]{1,0:T(8,128)S(1)} custom-call(f32[128,128]{1,0:T(8,128)S(1)} %slice.293), custom_call_target="Cholesky" | custom-call | tf_op jit(solution)/shard_map/cholesky/custom-call.1 | solution.py:22
  440.4 9.8 %custom-call.33 = f32[1,128,128]{1,2,0:T(8,128)S(1)} custom-call(f32[1,128,128]{2,1,0:T(8,128)S(1)} %fusion.102), custom_call_target="InvertDiagBlocksLowerTriangular" | custom-call | tf_op jit(solution)/shard_map/triangular_solve/custom-call.0 | solution.py:23
  453.7 11.7 %custom-call.34 = f32[128,128]{1,0:T(8,128)S(1)} custom-call(f32[128,128]{1,0:T(8,128)S(1)} %convolution_subtract_fusion.3), custom_call_target="Cholesky" | custom-call | tf_op jit(solution)/shard_map/cholesky/custom-call.1 | solution.py:22
  466.8 10.2 %custom-call.35 = f32[1,128,128]{1,2,0:T(8,128)S(1)} custom-call(f32[1,128,128]{2,1,0:T(8,128)S(1)} %fusion.103), custom_call_target="InvertDiagBlocksLowerTriangular" | custom-call | tf_op jit(solution)/shard_map/triangular_solve/custom-call.0 | solution.py:23
  479.0 1.9 constant_dynamic-update-slice_fusion.26
  486.8 1.3 fusion.24
  489.6 1.5 fusion.20
  492.5 2.2 fusion.18
  496.1 107.7 %reduce-scatter.2.cloned.1.call-done = f32[32,96,1024]{2,1,0:T(8,128)} async-done(((f32[128,96,1024]{2,1,0:T(8,128)}), f32[32,96,1024]{2,1,0:T(8,128)}) %reduce-scatter.2.cloned.1.call-update) | async-done | bytes 12582928 | tf_op jit(solution)/shard_map/reduce_scatter | solution.py:85
  603.9 1.4 fusion.87
  605.3 3.8 scatter-add.4
  609.0 1.3 slice.310
  610.4 6.7 fusion.93
  617.1 52.5 %fusion.9 = f32[32,96,1024]{2,0,1:T(8,128)} fusion(f32[32,96,1024]{2,1,0:T(8,128)} %scatter-add.4, f32[1024,1024]{1,0:T(8,128)} %maximum_dynamic-update-slice_fusion), kind=kOutput, calls=%fused_computation.11 | convolution fusion | flops 38654705664 | bytes 29360128 | tf_op jit(solution)/shard_map/dot_general | solution.py:98
  669.6 16.7 %copy.76 = f32[1,32,96,1024]{3,2,1,0:T(8,128)} copy(f32[1,32,96,1024]{3,1,2,0:T(8,128)} %bitcast.116) | data formatting | bytes 25165824
  686.4 33.3 %fusion.6 = f32[1,32,96,1024]{3,2,1,0:T(8,128)} fusion(f32[1,32,96,1024]{3,2,1,0:T(8,128)} %param.14, f32[1024,1024]{1,0:T(8,128)} %all-gather.8.cloned.1.call-done, f32[32,96,1024]{2,0,1:T(8,128)} %fusion.9), kind=kOutput, calls=%fused_computation.8 | convolution fusion | flops 19330498560 | bytes 41943040 | tf_op jit(solution)/shard_map/dot_general | solution.py:102
  (139 shorter events, 37.6 us)
Async XLA Ops:
  7.2 60.9 %all-gather.4.cloned.1.call-start = ((), (), s32[]{:S(2)}) async-start(), calls=%async_computation.1 | async-start | bytes 2359296 | tf_op jit(solution)/shard_map/all_gather | solution.py:64
  16.0 88.4 %all-reduce.9.cloned.1.call-start = ((), (), s32[]{:S(2)}) async-start(), calls=%async_computation.3 | async-start | bytes 1048576 | tf_op jit(solution)/shard_map/psum | solution.py:80
  17.2 87.2 %copy-start.18 = (f32[1024]{0:T(1024)S(1)}, f32[1024]{0:T(1024)}, u32[]{:S(2)}) copy-start(f32[1024]{0:T(1024)} %param.13) | copy-start | bytes 12292
  68.1 2.7 copy-start.20
  72.5 188.3 %all-gather.6.cloned.1.call-start = ((), (), s32[]{:S(2)}) async-start(), calls=%async_computation.4 | async-start | bytes 4718592 | tf_op jit(solution)/shard_map/all_gather | solution.py:82
  106.3 497.5 %reduce-scatter.2.cloned.1.call-start = ((), (), s32[]{:S(2)}) async-start(), calls=%async_computation.2 | async-start | bytes 62914560 | tf_op jit(solution)/shard_map/reduce_scatter | solution.py:85
  260.4 426.0 %all-gather.8.cloned.1.call-start = ((), (), s32[]{:S(2)}) async-start(), calls=%async_computation.5 | async-start | bytes 4325376 | tf_op jit(solution)/shard_map/all_gather | solution.py:97
  286.6 5.6 copy-start.1
  316.9 2.1 copy-start.3
  319.0 1.4 copy-start
  373.1 78.1 %copy-start.2 = (f32[896,128]{0,1:T(8,128)S(1)}, f32[896,128]{0,1:T(8,128)}, u32[]{:S(2)}) copy-start(f32[896,128]{0,1:T(8,128)} %copy-done.1) | copy-start | bytes 1376260
  373.1 78.8 %copy-start.4 = (f32[768,128]{0,1:T(8,128)S(1)}, f32[768,128]{0,1:T(8,128)}, u32[]{:S(2)}) copy-start(f32[768,128]{0,1:T(8,128)} %copy-done.3) | copy-start | bytes 1179652
  374.2 1.0 copy-start.5
  452.6 28.2 %copy-start.11 = (f32[128,128]{0,1:T(8,128)S(1)}, f32[128,128]{0,1:T(8,128)}, u32[]{:S(2)}) copy-start(f32[128,128]{0,1:T(8,128)} %get-tuple-element.29) | copy-start | bytes 196612
  452.6 28.2 %copy-start.12 = (f32[128,128]{0,1:T(8,128)S(1)}, f32[128,128]{0,1:T(8,128)}, u32[]{:S(2)}) copy-start(f32[128,128]{0,1:T(8,128)} %get-tuple-element.38) | copy-start | bytes 196612
  452.7 0.8 copy-start.8
  453.4 27.8 %copy-start.6 = (f32[128,896]{0,1:T(8,128)}, f32[128,896]{0,1:T(8,128)S(1)}, u32[]{:S(2)}) copy-start(f32[128,896]{0,1:T(8,128)S(1)} %get-tuple-element.77) | copy-start | bytes 1376260
  477.3 4.2 copy-start.17
  478.7 3.9 copy-start.10
  480.8 2.8 copy-start.16
  483.2 2.6 copy-start.14
  485.4 3.2 copy-start.13
  485.8 3.7 copy-start.9
  488.1 3.5 copy-start.15
  488.6 3.9 copy-start.7
  491.6 112.3 %copy-start.19 = (f32[1024]{0:T(1024)S(1)}, f32[1024]{0:T(1024)}, u32[]{:S(2)}) copy-start(f32[1024]{0:T(1024)} %param.13) | copy-start | bytes 12292
Sparse Core Ops, SparseCore 0:
  16.1 51.9 all-gather.3
  72.6 31.6 all-reduce.8
  107.1 73.3 all-gather.5
  260.5 343.3 reduce-scatter.1
  617.2 62.0 all-gather.7
